TPU v7x, 32 devices: a whole 2x2x4 slice. The times are simulated.
32 devices in a mesh: groups: 1, row: 32 (over z, y, x, core).
Axes of the slice: x: 2, y: 2, z: 4, core: 2. Of those that a mesh axis runs over, the one named last changes fastest.
Arguments:
- pair: bfloat16 [384, 384, 128], P(('groups', 'row')), may hold values from -6 to 6
- pair_mask: int32 [384, 384], P(('groups', 'row')), may hold values 0 or 1
- token_mask: int32 [384], P('groups'), may hold values 0 or 1
- proj_weights: bfloat16 [2, 128, 640], replicated, may hold values from -0.5 to 0.5
- out_weights: bfloat16 [2, 128, 128], replicated, may hold values from -0.5 to 0.5
Outputs:
- updated: bfloat16 [384, 384, 128], P(('groups', 'row'))
All inputs are finite; a program needn't handle non-finite values. No bound on the sum of `pair_mask` on one device may be relied on, other than what follows from the above.
Results may differ from a plain program's by a relative error of at most 0.0075.
Values may be sent and summed in bfloat16 or wider, within the bound.
A program may use at most 64 MiB of HBM per device.

v0:
```python
import jax
import jax.numpy as jnp
from jax import lax
from jax.sharding import PartitionSpec as P

EPS = 1e-05


def norm_axis(values, axis):
    mean = jnp.mean(values, axis=axis, keepdims=True)
    centred = values - mean
    var = jnp.mean(centred * centred, axis=axis, keepdims=True)
    return centred * lax.rsqrt(var + EPS)


def triangle_update(state, weights, out_w, mask, incoming):
    width = out_w.shape[0]
    owners = lax.axis_size("row")
    rows = state.shape[0]
    tokens = state.shape[1]
    normed = norm_axis(state.astype(jnp.float32), -1).astype(jnp.bfloat16)
    proj = jnp.einsum(
        "rnc,cd->drn", normed, weights[:, : 4 * width], preferred_element_type=jnp.float32
    )
    left = (mask[None] * jax.nn.sigmoid(proj[:width]) * proj[width : 2 * width]).astype(
        jnp.bfloat16
    )
    right = (mask[None] * jax.nn.sigmoid(proj[2 * width : 3 * width]) * proj[3 * width :]).astype(
        jnp.bfloat16
    )
    gate = jax.nn.sigmoid(
        jnp.einsum(
            "rnc,cd->rnd", normed, weights[:, 4 * width :], preferred_element_type=jnp.float32
        )
    )
    grouped_left = left.reshape(owners, width // owners, rows, tokens)
    grouped_right = right.reshape(owners, width // owners, rows, tokens)
    left_c = lax.all_to_all(grouped_left, "row", split_axis=0, concat_axis=2, tiled=True)
    right_c = lax.all_to_all(grouped_right, "row", split_axis=0, concat_axis=2, tiled=True)
    if incoming:
        product = jnp.einsum("gcki,gckj->gcij", left_c, right_c, preferred_element_type=jnp.float32)
    else:
        product = jnp.einsum("gcik,gcjk->gcij", left_c, right_c, preferred_element_type=jnp.float32)
    tri = product.astype(jnp.bfloat16)
    tri = tri.reshape(width // owners, tokens, tokens)
    tri_rows = lax.all_to_all(tri, "row", split_axis=1, concat_axis=0, tiled=True)
    tri_normed = norm_axis(tri_rows.astype(jnp.float32), 0).astype(jnp.bfloat16)
    out = jnp.einsum("crn,cd->rnd", tri_normed, out_w, preferred_element_type=jnp.float32)
    return (state.astype(jnp.float32) + gate * out).astype(jnp.bfloat16)


def on_device(pair, pair_mask, token_mask, proj_weights, out_weights):
    rows = pair.shape[0]
    offset = lax.axis_index("row") * rows
    tok_rows = lax.dynamic_slice_in_dim(token_mask, offset, rows).astype(jnp.float32)
    tok_cols = token_mask.astype(jnp.float32)
    mask = pair_mask.astype(jnp.float32) * tok_rows[:, None] * tok_cols[None, :]
    state = triangle_update(pair, proj_weights[0], out_weights[0], mask, False)
    state = triangle_update(state, proj_weights[1], out_weights[1], mask, True)
    return state


def solution(mesh):
    return jax.shard_map(
        on_device,
        mesh=mesh,
        in_specs=(
            P(("groups", "row"), None, None),
            P(("groups", "row"), None),
            P("groups"),
            P(),
            P(),
        ),
        out_specs=P(("groups", "row"), None, None),
        check_vma=False,
    )
```

profile of v0, /device:TPU:0, one launch (start us, length us, event | category | flops | bytes accessed | tf_op | source)
XLA Modules:
  0.0 242.4 jit_solution(8666336805016670573)
XLA Ops:
  0.0 1.8 copy.78
  7.8 2.5 %reshape.93 = bf16[32,4,12,384]{3,1,0,2:T(4,128)(2,1)S(1)} reshape(bf16[128,12,384]{2,0,1:T(8,128)(2,1)} %copy.83) | data formatting | bytes 2359296 | tf_op jit(solution)/shard_map/reshape | solution.py:36
  11.7 7.4 %all-to-all-start = ((bf16[32,4,12,384]{3,1,2,0:T(4,128)(2,1)}), bf16[32,4,12,384]{3,1,2,0:T(4,128)(2,1)}, u32[]{:S(2)}, u32[]{:S(2)}) async-start(bf16[32,4,12,384]{3,1,2,0:T(4,128)(2,1)} %copy.84), calls=%async_computation | async-start | bytes 2359296 | tf_op jit(solution)/shard_map/all_to_all | solution.py:38
  21.0 1.7 copy.86
  22.7 25.5 %all-to-all-done = bf16[32,4,12,384]{3,1,2,0:T(4,128)(2,1)} async-done(((bf16[32,4,12,384]{3,1,2,0:T(4,128)(2,1)}), bf16[32,4,12,384]{3,1,2,0:T(4,128)(2,1)}, u32[]{:S(2)}, u32[]{:S(2)}) %all-to-all-start) | async-done | bytes 1179680 | tf_op jit(solution)/shard_map/all_to_all | solution.py:38
  48.2 34.1 %all_to_all.78 = bf16[32,4,12,384]{3,1,2,0:T(4,128)(2,1)S(1)} all-to-all(bf16[32,4,12,384]{3,1,2,0:T(4,128)(2,1)S(1)} %copy.86), channel_id=1, replica_groups=mesh['groups'=1,'row'=32] {'row'}, dimensions={0} | all-to-all | bytes 2359296 | tf_op jit(solution)/shard_map/all_to_all | solution.py:39
  82.3 2.2 convolution_convert_fusion.1
  84.5 1.9 copy.89
  86.4 2.8 %all-to-all-start.2 = ((bf16[4,384,384]{2,0,1:T(4,128)(2,1)}), bf16[4,384,384]{2,0,1:T(4,128)(2,1)S(1)}, u32[]{:S(2)}, u32[]{:S(2)}) async-start(bf16[4,384,384]{2,0,1:T(4,128)(2,1)} %copy.89), calls=%async_computation.2 | async-start | bytes 2359296 | tf_op jit(solution)/shard_map/all_to_all | solution.py:46
  89.3 2.7 %fusion.47 = f32[12,384,128]{1,2,0:T(8,128)} fusion(bf16[12,384,128]{1,2,0:T(8,128)(2,1)S(1)} %copy.78, f32[12,384]{1,0:T(8,128)S(1)} %copy-done.10, f32[12,384]{1,0:T(8,128)S(1)} %copy-done.3, bf16[128,640]{0,1:T(8,128)(2,1)} %bitcast.105), kind=kOutput, calls=%fused_computation.66 | convolution fusion | flops 153354240 | bytes 3608576 | tf_op jit(solution)/shard_map/rnc,cd->rnd/dot_general | solution.py:32
  92.0 26.2 %all-to-all-done.2 = bf16[4,384,384]{2,0,1:T(4,128)(2,1)S(1)} async-done(((bf16[4,384,384]{2,0,1:T(4,128)(2,1)}), bf16[4,384,384]{2,0,1:T(4,128)(2,1)S(1)}, u32[]{:S(2)}, u32[]{:S(2)}) %all-to-all-start.2) | async-done | bytes 1179680 | tf_op jit(solution)/shard_map/all_to_all | solution.py:46
  120.9 2.7 %convert_reduce_fusion = (f32[12,384]{1,0:T(8,128)S(1)}, bf16[12,384,128]{1,2,0:T(8,128)(2,1)S(1)}) fusion(bf16[128,12,384]{2,0,1:T(8,128)(2,1)S(1)} %convert_element_type.97, bf16[2,128,128]{2,1,0:T(8,128)(2,1)} %param.9, f32[12,384,128]{1,2,0:T(8,128)} %fusion.47, bf16[12,384,128]{1,2,0:T(8,128)(2,1)S(1)} %copy.78), kind=kOutput, calls=%fused_computation.2 | convolution fusion | flops 156298752 | bytes 5949440 | tf_op jit(solution)/shard_map/crn,cd->rnd/dot_general | solution.py:48
  126.0 1.5 fusion.15
  128.9 2.5 %reshape.97 = bf16[32,4,12,384]{3,1,0,2:T(4,128)(2,1)S(1)} reshape(bf16[128,12,384]{2,0,1:T(8,128)(2,1)} %copy.95) | data formatting | bytes 2359296 | tf_op jit(solution)/shard_map/reshape | solution.py:36
  132.9 3.6 %all-to-all-start.3 = ((bf16[32,4,12,384]{3,1,2,0:T(4,128)(2,1)}), bf16[32,4,12,384]{3,1,2,0:T(4,128)(2,1)}, u32[]{:S(2)}, u32[]{:S(2)}) async-start(bf16[32,4,12,384]{3,1,2,0:T(4,128)(2,1)} %copy.96), calls=%async_computation.3 | async-start | bytes 2359296 | tf_op jit(solution)/shard_map/all_to_all | solution.py:38
  138.4 1.7 copy.98
  140.1 25.5 %all-to-all-done.3 = bf16[32,4,12,384]{3,1,2,0:T(4,128)(2,1)} async-done(((bf16[32,4,12,384]{3,1,2,0:T(4,128)(2,1)}), bf16[32,4,12,384]{3,1,2,0:T(4,128)(2,1)}, u32[]{:S(2)}, u32[]{:S(2)}) %all-to-all-start.3) | async-done | bytes 1179680 | tf_op jit(solution)/shard_map/all_to_all | solution.py:38
  165.6 34.1 %all_to_all.79 = bf16[32,4,12,384]{3,1,2,0:T(4,128)(2,1)S(1)} all-to-all(bf16[32,4,12,384]{3,1,2,0:T(4,128)(2,1)S(1)} %copy.98), channel_id=1, replica_groups=mesh['groups'=1,'row'=32] {'row'}, dimensions={0} | all-to-all | bytes 2359296 | tf_op jit(solution)/shard_map/all_to_all | solution.py:39
  199.7 2.2 convolution_convert_fusion
  201.9 1.9 copy.101
  203.9 2.9 %all-to-all-start.5 = ((bf16[4,384,384]{2,0,1:T(4,128)(2,1)}), bf16[4,384,384]{2,0,1:T(4,128)(2,1)S(1)}, u32[]{:S(2)}, u32[]{:S(2)}) async-start(bf16[4,384,384]{2,0,1:T(4,128)(2,1)} %copy.101), calls=%async_computation.5 | async-start | bytes 2359296 | tf_op jit(solution)/shard_map/all_to_all | solution.py:46
  206.8 2.7 %fusion.50 = f32[12,384,128]{1,2,0:T(8,128)} fusion(bf16[12,384,128]{1,2,0:T(8,128)(2,1)S(1)} %get-tuple-element.12, f32[12,384]{1,0:T(8,128)S(1)} %copy-done.12, f32[12,384]{1,0:T(8,128)S(1)} %copy-done.5, bf16[128,640]{1,0:T(8,128)(2,1)} %get-tuple-element.9), kind=kOutput, calls=%fused_computation.67 | convolution fusion | flops 153354240 | bytes 3608576 | tf_op jit(solution)/shard_map/rnc,cd->rnd/dot_general | solution.py:32
  209.5 26.1 %all-to-all-done.5 = bf16[4,384,384]{2,0,1:T(4,128)(2,1)S(1)} async-done(((bf16[4,384,384]{2,0,1:T(4,128)(2,1)}), bf16[4,384,384]{2,0,1:T(4,128)(2,1)S(1)}, u32[]{:S(2)}, u32[]{:S(2)}) %all-to-all-start.5) | async-done | bytes 1179680 | tf_op jit(solution)/shard_map/all_to_all | solution.py:46
  238.4 2.6 %fusion.9 = bf16[12,384,128]{1,2,0:T(8,128)(2,1)S(1)} fusion(bf16[12,384,128]{1,2,0:T(8,128)(2,1)S(1)} %get-tuple-element.12, f32[12,384,128]{1,2,0:T(8,128)} %fusion.50, bf16[128,12,384]{2,0,1:T(8,128)(2,1)S(1)} %convert_element_type.108, bf16[2,128,128]{2,1,0:T(8,128)(2,1)} %param.9), kind=kOutput, calls=%fused_computation.17 | convolution fusion | flops 155123712 | bytes 5931008 | tf_op jit(solution)/shard_map/crn,cd->rnd/dot_general | solution.py:48
  (68 shorter events, 23.3 us)
Async XLA Ops:
  0.0 2.4 copy-start.6
  0.0 3.2 %copy-start.14 = (s32[384]{0:T(512)S(1)}, s32[384]{0:T(512)}, u32[]{:S(2)}) copy-start(s32[384]{0:T(512)} %param.7) | copy-start | bytes 4612
  2.0 2.8 %copy-start.2 = (f32[12,384]{1,0:T(8,128)}, f32[12,384]{1,0:T(8,128)S(1)}, u32[]{:S(2)}) copy-start(f32[12,384]{1,0:T(8,128)S(1)} %broadcast_multiply_fusion.3) | copy-start | bytes 55300
  2.4 2.4 copy-start.9
  3.2 1.6 copy-start.1
  3.3 1.5 copy-start.13
  4.9 1.5 copy-start.7
  11.7 36.5 %all-to-all-start = ((bf16[32,4,12,384]{3,1,2,0:T(4,128)(2,1)}), bf16[32,4,12,384]{3,1,2,0:T(4,128)(2,1)}, u32[]{:S(2)}, u32[]{:S(2)}) async-start(bf16[32,4,12,384]{3,1,2,0:T(4,128)(2,1)} %copy.84), calls=%async_computation | async-start | bytes 2359296 | tf_op jit(solution)/shard_map/all_to_all | solution.py:38
  84.5 4.8 %copy-start.3 = (f32[12,384]{1,0:T(8,128)S(1)}, f32[12,384]{1,0:T(8,128)}, u32[]{:S(2)}) copy-start(f32[12,384]{1,0:T(8,128)} %copy-done.2) | copy-start | bytes 55300
  84.5 4.8 %copy-start.10 = (f32[12,384]{1,0:T(8,128)S(1)}, f32[12,384]{1,0:T(8,128)}, u32[]{:S(2)}) copy-start(f32[12,384]{1,0:T(8,128)} %copy-done.9) | copy-start | bytes 55300
  86.4 31.7 %all-to-all-start.2 = ((bf16[4,384,384]{2,0,1:T(4,128)(2,1)}), bf16[4,384,384]{2,0,1:T(4,128)(2,1)S(1)}, u32[]{:S(2)}, u32[]{:S(2)}) async-start(bf16[4,384,384]{2,0,1:T(4,128)(2,1)} %copy.89), calls=%async_computation.2 | async-start | bytes 2359296 | tf_op jit(solution)/shard_map/all_to_all | solution.py:46
  120.9 3.7 %copy-start = (bf16[128,640]{1,0:T(8,128)(2,1)S(1)}, bf16[128,640]{1,0:T(8,128)(2,1)}, u32[]{:S(2)}) copy-start(bf16[128,640]{1,0:T(8,128)(2,1)} %get-tuple-element.9) | copy-start | bytes 491524
  123.6 0.6 copy-start.4
  124.0 0.6 copy-start.11
  124.6 1.4 copy-start.8
  132.9 32.7 %all-to-all-start.3 = ((bf16[32,4,12,384]{3,1,2,0:T(4,128)(2,1)}), bf16[32,4,12,384]{3,1,2,0:T(4,128)(2,1)}, u32[]{:S(2)}, u32[]{:S(2)}) async-start(bf16[32,4,12,384]{3,1,2,0:T(4,128)(2,1)} %copy.96), calls=%async_computation.3 | async-start | bytes 2359296 | tf_op jit(solution)/shard_map/all_to_all | solution.py:38
  201.9 4.8 %copy-start.5 = (f32[12,384]{1,0:T(8,128)S(1)}, f32[12,384]{1,0:T(8,128)}, u32[]{:S(2)}) copy-start(f32[12,384]{1,0:T(8,128)} %copy-done.4) | copy-start | bytes 55300
  201.9 4.8 %copy-start.12 = (f32[12,384]{1,0:T(8,128)S(1)}, f32[12,384]{1,0:T(8,128)}, u32[]{:S(2)}) copy-start(f32[12,384]{1,0:T(8,128)} %copy-done.11) | copy-start | bytes 55300
  203.9 31.7 %all-to-all-start.5 = ((bf16[4,384,384]{2,0,1:T(4,128)(2,1)}), bf16[4,384,384]{2,0,1:T(4,128)(2,1)S(1)}, u32[]{:S(2)}, u32[]{:S(2)}) async-start(bf16[4,384,384]{2,0,1:T(4,128)(2,1)} %copy.101), calls=%async_computation.5 | async-start | bytes 2359296 | tf_op jit(solution)/shard_map/all_to_all | solution.py:46
where the time goes:
time: 243 us; the launch traced here: 242 us
  waiting for transfers between devices  103 us (42%)
  blocking collectives  68.2 us (28%)
  local copies, waits for them, and re-layouts  28 us (12%)
  matrix products  17.9 us (7%)
  starting transfers between devices  16.8 us (7%)
  other arithmetic  7.79 us (3%)
    all_to_all x2, blocking collectives, triangle_update(): lax.all_to_all(grouped_right, 'row', split_axis=0, concat_axis=2, tiled=T...  68.2 us
    all_to_all x2, waiting for transfers between devices, triangle_update(): lax.all_to_all(tri, 'row', split_axis=1, concat_axis=0, tiled=True)  52.3 us
    all_to_all x2, waiting for transfers between devices, triangle_update(): lax.all_to_all(grouped_left, 'row', split_axis=0, concat_axis=2, tiled=True)  50.9 us
    all_to_all x2, starting transfers between devices, triangle_update(): lax.all_to_all(grouped_left, 'row', split_axis=0, concat_axis=2, tiled=True)  11.1 us
    reshape x4, local copies, waits for them, and re-layouts, triangle_update(): grouped_left = left.reshape(owners, width // owners, rows, tokens)  7.83 us
    all_to_all x2, starting transfers between devices, triangle_update(): lax.all_to_all(tri, 'row', split_axis=1, concat_axis=0, tiled=True)  5.71 us
    reshape x4, local copies, waits for them, and re-layouts, triangle_update(): grouped_right = right.reshape(owners, width // owners, rows, tokens)  5.68 us
    dot_general x2, matrix products, triangle_update(): jnp.einsum('rnc,cd->rnd', normed, weights[:, 4 * width:], preferred_eleme...  5.37 us
  transfers between devices with their start and end apart: 4, of which 4 were waited for; matrix products, arithmetic and copies ran while one was open for 5% of the time, Pallas kernels for 0%

commit v1 on v0

v1 whole, which is shorter than its diff:
```python
import functools

import jax
import jax.numpy as jnp
from jax import lax
from jax.experimental import pallas as pl
from jax.experimental.pallas import tpu as pltpu
from jax.sharding import PartitionSpec as P

EPS = 1e-05
MESH = pl.DeviceIdType.MESH


def norm_axis(values, axis):
    mean = jnp.mean(values, axis=axis, keepdims=True)
    centred = values - mean
    var = jnp.mean(centred * centred, axis=axis, keepdims=True)
    return centred * lax.rsqrt(var + EPS)


def dot(a, b, dims):
    return lax.dot_general(a, b, (dims, ((), ())), preferred_element_type=jnp.float32)


def exchange_kernel(n, kinds, *refs):
    m = len(kinds)
    srcs, outs = refs[:m], refs[m : 2 * m]
    send_sem, recv_sem, own_sem = refs[2 * m :]
    h = n // 2
    g = lax.axis_index("groups")
    me = lax.axis_index("row")
    half, q, core = me // h, me % h, me % 2
    wide = any(kind != "half" for kind in kinds)
    barrier = pltpu.get_barrier_semaphore()

    def greet(base, s):
        pl.semaphore_signal(
            barrier, inc=1, device_id=(g, base * h + (q + s) % h), device_id_type=MESH
        )

    def greet_near(s, carry):
        greet(half, s)
        return carry

    def greet_far(s, carry):
        greet(1 - half, s)
        return carry

    lax.fori_loop(1, h, greet_near, 0)
    if wide:
        lax.fori_loop(0, h, greet_far, 0)
    pl.semaphore_wait(barrier, (n if wide else h) - 1)

    def send(i, block, slot, dest):
        pltpu.make_async_remote_copy(
            src_ref=srcs[i].at[block],
            dst_ref=outs[i].at[slot],
            send_sem=send_sem.at[i],
            recv_sem=recv_sem.at[i],
            device_id=(g, dest),
            device_id_type=MESH,
        ).start()

    def far(to):
        dest = (1 - half) * h + to
        for i, kind in enumerate(kinds):
            if kind != "half":
                send(i, to if kind == "both" else dest, me, dest)

    def near(to):
        dest = half * h + to

        @pl.when(to != q)
        def _():
            for i, kind in enumerate(kinds):
                send(i, dest if kind == "all" else to, q if kind == "half" else me, dest)

    def step(s, carry):
        to = (q + s) % h if h & (h - 1) else q ^ s ^ (core * (h - 2))
        if wide:
            far(to)
        near(to)
        return carry

    lax.fori_loop(0, h, step, 0)
    own = []
    for i, kind in enumerate(kinds):
        copy = pltpu.make_async_copy(
            srcs[i].at[me if kind == "all" else q],
            outs[i].at[q if kind == "half" else me],
            own_sem.at[i],
        )
        copy.start()
        own.append(copy)
    for copy in own:
        copy.wait()
    for i, kind in enumerate(kinds):
        got = outs[i].at[pl.ds(0, (h if kind == "half" else n) - 1)]
        pltpu.make_async_copy(got, got, recv_sem.at[i]).wait()
        pltpu.make_async_copy(got, got, send_sem.at[i]).wait()


def exchange(n, kinds, ident, *srcs):
    m = len(kinds)
    shapes = [
        jax.ShapeDtypeStruct((n // 2 if kind == "half" else n,) + src.shape[1:], src.dtype)
        for kind, src in zip(kinds, srcs)
    ]
    return pl.pallas_call(
        functools.partial(exchange_kernel, n, kinds),
        out_shape=shapes,
        in_specs=[pl.BlockSpec(memory_space=pl.ANY)] * m,
        out_specs=[pl.BlockSpec(memory_space=pl.ANY)] * m,
        scratch_shapes=[pltpu.SemaphoreType.DMA((m,))] * 3,
        compiler_params=pltpu.CompilerParams(collective_id=ident, has_side_effects=True),
    )(*srcs)


def normed_row(state_ref, r):
    return norm_axis(state_ref[r].astype(jnp.float32), -1).astype(jnp.bfloat16)


def project_row(normed, w_ref, mask_ref, left_ref, right_ref, r):
    owners, _, share, _ = left_ref.shape
    width = owners * share
    mask = mask_ref[pl.ds(r, 1), :]
    for lo, out_ref in ((0, left_ref), (2 * width, right_ref)):
        proj = dot(w_ref[:, lo : lo + 2 * width], normed, ((0,), (1,)))
        side = (mask * jax.nn.sigmoid(proj[:width]) * proj[width:]).astype(out_ref.dtype)
        for owner in range(owners):
            out_ref[owner, r] = side[owner * share : (owner + 1) * share]


def finish_row(state_ref, normed, w_ref, wo_ref, tri_ref, r):
    sources, _, share, tokens = tri_ref.shape
    width = wo_ref.shape[0]
    owners = width // share
    tri = jnp.concatenate([tri_ref[s, r].astype(jnp.float32) for s in range(owners)], axis=0)
    if sources > owners:
        tri += jnp.concatenate(
            [tri_ref[s, r].astype(jnp.float32) for s in range(owners, sources)], axis=0
        )
    tri_normed = norm_axis(tri, 0).astype(jnp.bfloat16)
    out = dot(tri_normed, wo_ref[...], ((0,), (0,)))
    gate = jax.nn.sigmoid(dot(normed, w_ref[:, 4 * width :], ((1,), (0,))))
    return (state_ref[r].astype(jnp.float32) + gate * out).astype(jnp.bfloat16)


def first_kernel(state_ref, mask_ref, w_ref, left_ref, right_ref):
    def row(r, carry):
        project_row(normed_row(state_ref, r), w_ref, mask_ref, left_ref, right_ref, r)
        return carry

    lax.fori_loop(0, state_ref.shape[0], row, 0)


def middle_kernel(
    state_ref, mask_ref, w_ref, wo_ref, w_next_ref, tri_ref, next_ref, left_ref, right_ref
):
    def row(r, carry):
        next_ref[r] = finish_row(
            state_ref, normed_row(state_ref, r), w_ref, wo_ref, tri_ref, r
        )
        project_row(normed_row(next_ref, r), w_next_ref, mask_ref, left_ref, right_ref, r)
        return carry

    lax.fori_loop(0, state_ref.shape[0], row, 0)


def last_kernel(state_ref, w_ref, wo_ref, tri_ref, next_ref):
    def row(r, carry):
        next_ref[r] = finish_row(
            state_ref, normed_row(state_ref, r), w_ref, wo_ref, tri_ref, r
        )
        return carry

    lax.fori_loop(0, state_ref.shape[0], row, 0)


def local(body, out_shape, *args):
    vmem = pl.BlockSpec(memory_space=pltpu.VMEM)
    return pl.pallas_call(
        body,
        out_shape=out_shape,
        in_specs=[vmem] * len(args),
        out_specs=jax.tree.map(lambda _: vmem, out_shape),
        compiler_params=pltpu.CompilerParams(vmem_limit_bytes=40 * 2**20),
    )(*args)


def on_device(pair, pair_mask, token_mask, proj_weights, out_weights):
    rows, tokens, _ = pair.shape
    n = lax.axis_size("row")
    h = n // 2
    share = out_weights.shape[1] // h
    offset = lax.axis_index("row") * rows
    tok_rows = lax.dynamic_slice_in_dim(token_mask, offset, rows).astype(jnp.float32)
    tok_cols = token_mask.astype(jnp.float32)
    mask = pair_mask.astype(jnp.float32) * tok_rows[:, None] * tok_cols[None, :]
    side = jax.ShapeDtypeStruct((h, rows, share, tokens), jnp.bfloat16)
    state_shape = jax.ShapeDtypeStruct(pair.shape, pair.dtype)

    left, right = local(first_kernel, [side, side], pair, mask, proj_weights[0])
    left, right = exchange(n, ("half", "both"), 1, left, right)
    tri = jnp.einsum("srck,tuck->srctu", left, right, preferred_element_type=jnp.float32)
    tri = tri.astype(jnp.bfloat16).reshape(h, rows, share, tokens)
    (tri,) = exchange(n, ("half",), 2, tri)
    state, left, right = local(
        middle_kernel,
        [state_shape, side, side],
        pair,
        mask,
        proj_weights[0],
        out_weights[0],
        proj_weights[1],
        tri,
    )
    left, right = exchange(n, ("half", "half"), 3, left, right)
    tri = jnp.einsum("srci,srcj->icj", left, right, preferred_element_type=jnp.float32)
    tri = tri.astype(jnp.bfloat16).reshape(n, rows, share, tokens)
    (tri,) = exchange(n, ("all",), 4, tri)
    return local(last_kernel, state_shape, state, proj_weights[1], out_weights[1], tri)


def solution(mesh):
    return jax.shard_map(
        on_device,
        mesh=mesh,
        in_specs=(
            P(("groups", "row"), None, None),
            P(("groups", "row"), None),
            P("groups"),
            P(),
            P(),
        ),
        out_specs=P(("groups", "row"), None, None),
        check_vma=False,
    )
```

time: 243 us -> 248 us (1.021)
  Pallas kernels: 0 us -> 185 us
  waiting for transfers between devices: 103 us -> 0 us
  blocking collectives: 68.2 us -> 0 us
  local copies, waits for them, and re-layouts: 28 us -> 49.7 us
  starting transfers between devices: 16.8 us -> 0 us
  matrix products: 17.9 us -> 10.8 us
  other arithmetic: 7.79 us -> 2.25 us
    pallas_call x0 -> x7, Pallas kernels: none -> 185 us  [the longest x4 163 us: exchange(): pl.pallas_call(functools.partial(exchange_kernel, n, kinds), out_shape=sh...]
    all_to_all x4 -> x0, waiting for transfers between devices: 103 us -> none  [the longest x2 52.3 us: triangle_update(): lax.all_to_all(tri, 'row', split_axis=1, concat_axis=0, tiled=True)]
    all_to_all x2 -> x0, blocking collectives: 68.2 us -> none  [triangle_update(): lax.all_to_all(grouped_right, 'row', split_axis=0, concat_axis=2, tiled=T...]
    all_to_all x4 -> x0, starting transfers between devices: 16.8 us -> none  [the longest x2 11.1 us: triangle_update(): lax.all_to_all(grouped_left, 'row', split_axis=0, concat_axis=2, tiled=True)]
    reshape x8 -> x1, local copies, waits for them, and re-layouts: 13.5 us -> 22.8 us  [on_device(): tri = tri.astype(jnp.bfloat16).reshape(h, rows, share, tokens)]
    dot_general x8 -> x2, matrix products: 17.9 us -> 10.8 us  [the longest x1 7.25 us: on_device(): jnp.einsum('srck,tuck->srctu', left, right, preferred_element_type=jnp.fl...]
    convert_element_type x11 -> x2, local copies, waits for them, and re-layouts: 11.2 us -> 17.6 us  [the longest x1 14.8 us: on_device(): tri = tri.astype(jnp.bfloat16).reshape(h, rows, share, tokens)]
    unnamed x32 -> x18, local copies, waits for them, and re-layouts: 2.57 us -> 8.28 us
  transfers between devices with their start and end apart: 4 -> 0, of which waited for: 4 -> 0; matrix products, arithmetic and copies ran while one was open for 5% -> 0% of each run, Pallas kernels for 0% -> 0%
where the time goes in v1:
time: 248 us
  Pallas kernels  185 us (75%)
  local copies, waits for them, and re-layouts  49.7 us (20%)
  matrix products  10.8 us (4%)
    pallas_call x4, Pallas kernels, exchange(): pl.pallas_call(functools.partial(exchange_kernel, n, kinds), out_shape=sh...  163 us
    reshape x1, local copies, waits for them, and re-layouts, on_device(): tri = tri.astype(jnp.bfloat16).reshape(h, rows, share, tokens)  22.8 us
    pallas_call x3, Pallas kernels, local(): pl.pallas_call(body, out_shape=out_shape, in_specs=[vmem] * len(args), ou...  22.1 us
    convert_element_type x1, local copies, waits for them, and re-layouts, on_device(): tri = tri.astype(jnp.bfloat16).reshape(h, rows, share, tokens)  14.8 us
    unnamed x18, local copies, waits for them, and re-layouts  8.28 us
    dot_general x1, matrix products, on_device(): jnp.einsum('srck,tuck->srctu', left, right, preferred_element_type=jnp.fl...  7.25 us

profile of v1, /device:TPU:0, one launch (start us, length us, event | category | flops | bytes accessed | tf_op | source)
XLA Modules:
  0.0 247.8 jit_solution(14430269058738655619)
XLA Ops:
  0.0 0.8 dynamic-slice_convert_fusion
  0.8 0.7 convert_element_type.23
  1.4 0.8 multiply_multiply_fusion.mask_ref
  2.2 1.0 slice_bitcast_fusion
  3.3 1.3 copy-done.1
  4.6 5.4 %shard_map.55 = (bf16[16,12,8,384]{3,2,1,0:T(8,128)(2,1)S(1)}, bf16[16,12,8,384]{3,2,1,0:T(8,128)(2,1)S(1)}) custom-call(bf16[12,384,128]{2,1,0:T(8,128)(2,1)S(1)} %copy-done.1, f32[12,384]{1,0:T(8,128)S(1)} %multiply_multiply_fusion.mask_ref, bf16[128,640]{1,0:T(8,128)(2,1)S(1)} %get-tuple-element.24.w_ref), custom_call_target="tpu_custom_call" | custom-call | tf_op jit(solution)/shard_map/pallas_call | solution.py:182
  10.0 0.0 copy-start.6
  10.0 1.0 copy-done.6
  11.0 1.0 copy-done.7
  12.0 59.4 %shard_map.56 = (bf16[16,12,8,384]{3,2,1,0:T(8,128)(2,1)}, bf16[32,12,8,384]{3,2,1,0:T(8,128)(2,1)}) custom-call(bf16[16,12,8,384]{3,2,1,0:T(8,128)(2,1)} %copy-done.6, bf16[16,12,8,384]{3,2,1,0:T(8,128)(2,1)} %copy-done.7), custom_call_target="tpu_custom_call" | custom-call | tf_op jit(solution)/shard_map/pallas_call | solution.py:109
  71.5 7.3 %convert_bitcast_fusion = bf16[16,12,8,32,12]{3,0,1,4,2:T(8,128)(2,1)} fusion(bf16[32,12,8,384,1]{3,2,1,0,4:T(8,128)(2,1)} %bitcast.23, bf16[16,12,8,384,1]{3,2,1,0,4:T(8,128)(2,1)} %bitcast.24), kind=kOutput, calls=%fused_computation.1 | convolution fusion | flops 453574656 | bytes 4718592 | tf_op jit(solution)/shard_map/srck,tuck->srctu/dot_general | solution.py:205
  78.7 14.8 %copy.14 = bf16[16,12,8,32,12]{4,3,2,1,0:T(8,128)(2,1)} copy(bf16[16,12,8,32,12]{3,0,1,4,2:T(8,128)(2,1)} %convert_bitcast_fusion) | data formatting | bytes 2359296 | tf_op jit(solution)/shard_map/convert_element_type | solution.py:206
  93.5 22.8 %reshape.8.refs_0_ = bf16[16,12,8,384]{3,2,1,0:T(8,128)(2,1)} reshape(bf16[16,12,8,32,12]{4,3,2,1,0:T(8,128)(2,1)} %copy.14) | data formatting | bytes 2359296 | tf_op jit(solution)/shard_map/reshape | solution.py:206
  116.3 17.1 %shard_map.57.tri_ref = bf16[16,12,8,384]{3,2,1,0:T(8,128)(2,1)} custom-call(bf16[16,12,8,384]{3,2,1,0:T(8,128)(2,1)} %reshape.8.refs_0_), custom_call_target="tpu_custom_call" | custom-call | tf_op jit(solution)/shard_map/pallas_call | solution.py:109
  133.4 1.3 copy-done.3
  134.7 11.1 %shard_map.58 = (bf16[12,384,128]{2,1,0:T(8,128)(2,1)S(1)}, bf16[16,12,8,384]{3,2,1,0:T(8,128)(2,1)S(1)}, bf16[16,12,8,384]{3,2,1,0:T(8,128)(2,1)S(1)}) custom-call(bf16[12,384,128]{2,1,0:T(8,128)(2,1)S(1)} %copy-done.2, f32[12,384]{1,0:T(8,128)S(1)} %multiply_multiply_fusion.mask_ref, bf16[128,640]{1,0:T(8,128)(2,1)S(1)} %get-tuple-element.24.w_ref, ...), custom_call_target="tpu_custom_call" | custom-call | tf_op jit(solution)/shard_map/pallas_call | solution.py:182
  145.8 1.0 copy-done.4
  146.8 1.0 copy-done.5
  147.9 29.9 %shard_map.59 = (bf16[16,12,8,384]{3,2,1,0:T(8,128)(2,1)}, bf16[16,12,8,384]{3,2,1,0:T(8,128)(2,1)}) custom-call(bf16[16,12,8,384]{3,2,1,0:T(8,128)(2,1)} %copy-done.4, bf16[16,12,8,384]{3,2,1,0:T(8,128)(2,1)} %copy-done.5), custom_call_target="tpu_custom_call" | custom-call | tf_op jit(solution)/shard_map/pallas_call | solution.py:109
  177.8 3.5 %fusion = bf16[384,8,384]{2,0,1:T(8,128)(2,1)S(1)} fusion(bf16[16,12,8,384]{3,2,1,0:T(8,128)(2,1)} %get-tuple-element.22, bf16[16,12,8,384]{3,2,1,0:T(8,128)(2,1)} %get-tuple-element.21), kind=kOutput, calls=%fused_computation.2 | convolution fusion | flops 454164480 | bytes 4718592 | tf_op jit(solution)/shard_map/srci,srcj->icj/dot_general | solution.py:219
  181.3 2.8 %copy.17 = bf16[384,8,384]{2,1,0:T(8,128)(2,1)} copy(bf16[384,8,384]{2,0,1:T(8,128)(2,1)S(1)} %fusion) | data formatting | bytes 4718592 | tf_op jit(solution)/shard_map/convert_element_type | solution.py:220
  184.1 56.3 %shard_map.60.tri_ref = bf16[32,12,8,384]{3,2,1,0:T(8,128)(2,1)} custom-call(bf16[32,12,8,384]{3,2,1,0:T(8,128)(2,1)} %bitcast.22), custom_call_target="tpu_custom_call" | custom-call | tf_op jit(solution)/shard_map/pallas_call | solution.py:109
  240.5 1.7 copy-done
  242.2 5.6 %shard_map.61 = bf16[12,384,128]{2,1,0:T(8,128)(2,1)} custom-call(bf16[12,384,128]{2,1,0:T(8,128)(2,1)S(1)} %get-tuple-element.18.state_ref, bf16[128,640]{1,0:T(8,128)(2,1)S(1)} %get-tuple-element.23.w_next_ref.w_ref, bf16[128,128]{1,0:T(8,128)(2,1)S(1)} %get-tuple-element.25.wo_ref, bf16[32,12,8,384]{3,2,1,0:T(8,128)(2,1)S(1)} %copy-done), custom_call_target="tpu_custom_call" | custom-call | tf_op jit(solution)/shard_map/pallas_call | solution.py:182
  (11 shorter events, 0.0 us)
Async XLA Ops:
  3.3 1.3 copy-start.1
  10.0 1.0 copy-start.6
  11.0 1.0 copy-start.7
  116.3 17.1 %copy-start.8 = (bf16[2,128,128]{2,1,0:T(8,128)(2,1)S(1)}, bf16[2,128,128]{2,1,0:T(8,128)(2,1)}, u32[]{:S(2)}) copy-start(bf16[2,128,128]{2,1,0:T(8,128)(2,1)} %param.9) | copy-start | bytes 196612
  116.3 17.1 %copy-start.2 = (bf16[12,384,128]{2,1,0:T(8,128)(2,1)S(1)}, bf16[12,384,128]{2,1,0:T(8,128)(2,1)}, u32[]{:S(2)}) copy-start(bf16[12,384,128]{2,1,0:T(8,128)(2,1)} %state_ref.3) | copy-start | bytes 3538948
  133.4 1.3 copy-start.3
  145.8 1.0 copy-start.4
  146.8 1.0 copy-start.5
  240.5 1.7 copy-start

commit v2 on v1

--- a/solution.py
+++ b/solution.py
@@ -109,8 +109,8 @@
     return pl.pallas_call(
         functools.partial(exchange_kernel, n, kinds),
         out_shape=shapes,
-        in_specs=[pl.BlockSpec(memory_space=pl.ANY)] * m,
-        out_specs=[pl.BlockSpec(memory_space=pl.ANY)] * m,
+        in_specs=[pl.BlockSpec(memory_space=pltpu.VMEM)] * m,
+        out_specs=[pl.BlockSpec(memory_space=pltpu.VMEM)] * m,
         scratch_shapes=[pltpu.SemaphoreType.DMA((m,))] * 3,
         compiler_params=pltpu.CompilerParams(collective_id=ident, has_side_effects=True),
     )(*srcs)
@@ -202,7 +202,9 @@
 
     left, right = local(first_kernel, [side, side], pair, mask, proj_weights[0])
     left, right = exchange(n, ("half", "both"), 1, left, right)
-    tri = jnp.einsum("srck,tuck->srctu", left, right, preferred_element_type=jnp.float32)
+    left = left.reshape(h * rows, share, tokens)
+    right = right.reshape(tokens, share, tokens)
+    tri = jnp.einsum("ick,jck->icj", left, right, preferred_element_type=jnp.float32)
     tri = tri.astype(jnp.bfloat16).reshape(h, rows, share, tokens)
     (tri,) = exchange(n, ("half",), 2, tri)
     state, left, right = local(

time: 248 us -> 219 us (0.88)
  local copies, waits for them, and re-layouts: 49.7 us -> 13.8 us
  Pallas kernels: 185 us -> 195 us
  matrix products: 10.8 us -> 6.59 us
    reshape x1 -> x0, local copies, waits for them, and re-layouts: 22.8 us -> none  [on_device(): tri = tri.astype(jnp.bfloat16).reshape(h, rows, share, tokens)]
    convert_element_type x1, local copies, waits for them, and re-layouts: 14.8 us -> 1.7 us  [on_device(): tri = tri.astype(jnp.bfloat16).reshape(h, rows, share, tokens)]
    pallas_call x4, Pallas kernels: 163 us -> 173 us  [exchange(): pl.pallas_call(functools.partial(exchange_kernel, n, kinds), out_shape=sh...]
    dot_general x1, matrix products: 7.25 us -> 3.05 us  [on_device(): jnp.einsum('ick,jck->icj', left, right, preferred_element_type=jnp.float32)]
where the time goes in v2:
time: 219 us; the launch traced here: 218 us
  Pallas kernels  195 us (89%)
  local copies, waits for them, and re-layouts  13.8 us (6%)
  matrix products  6.59 us (3%)
  other arithmetic  2.25 us (1%)
    pallas_call x4, Pallas kernels, exchange(): pl.pallas_call(functools.partial(exchange_kernel, n, kinds), out_shape=sh...  173 us
    pallas_call x3, Pallas kernels, local(): pl.pallas_call(body, out_shape=out_shape, in_specs=[vmem] * len(args), ou...  22.1 us
    unnamed x18, local copies, waits for them, and re-layouts  8.28 us

profile of v2, /device:TPU:0, one launch (start us, length us, event | category | flops | bytes accessed | tf_op | source)
XLA Modules:
  0.0 218.2 jit_solution(5640543027096380838)
XLA Ops:
  0.0 0.8 dynamic-slice_convert_fusion
  0.8 0.7 convert_element_type.23
  1.4 0.8 multiply_multiply_fusion.mask_ref
  2.2 1.0 slice_bitcast_fusion
  3.3 0.0 copy-start.1
  3.3 1.3 copy-done.1
  4.6 5.4 %shard_map.55 = (bf16[16,12,8,384]{3,2,1,0:T(8,128)(2,1)S(1)}, bf16[16,12,8,384]{3,2,1,0:T(8,128)(2,1)S(1)}) custom-call(bf16[12,384,128]{2,1,0:T(8,128)(2,1)S(1)} %copy-done.1, f32[12,384]{1,0:T(8,128)S(1)} %multiply_multiply_fusion.mask_ref, bf16[128,640]{1,0:T(8,128)(2,1)S(1)} %get-tuple-element.24.w_ref), custom_call_target="tpu_custom_call" | custom-call | tf_op jit(solution)/shard_map/pallas_call | solution.py:182
  10.0 0.0 copy-start.6
  10.0 1.0 copy-done.6
  11.0 1.0 copy-done.7
  12.0 62.5 %shard_map.56 = (bf16[16,12,8,384]{3,2,1,0:T(8,128)(2,1)}, bf16[32,12,8,384]{3,2,1,0:T(8,128)(2,1)}) custom-call(bf16[16,12,8,384]{3,2,1,0:T(8,128)(2,1)} %copy-done.6, bf16[16,12,8,384]{3,2,1,0:T(8,128)(2,1)} %copy-done.7), custom_call_target="tpu_custom_call" | custom-call | tf_op jit(solution)/shard_map/pallas_call | solution.py:109
  74.5 3.1 %fusion.6 = bf16[192,8,384]{2,0,1:T(8,128)(2,1)S(1)} fusion(bf16[384,8,384]{2,1,0:T(8,128)(2,1)} %bitcast.23, bf16[192,8,384]{2,1,0:T(8,128)(2,1)} %bitcast.24), kind=kOutput, calls=%fused_computation.5 | convolution fusion | flops 453574656 | bytes 4718592 | tf_op jit(solution)/shard_map/ick,jck->icj/dot_general | solution.py:207
  77.6 1.7 copy.8
  79.3 19.1 %shard_map.57.tri_ref = bf16[16,12,8,384]{3,2,1,0:T(8,128)(2,1)} custom-call(bf16[16,12,8,384]{3,2,1,0:T(8,128)(2,1)} %bitcast.22), custom_call_target="tpu_custom_call" | custom-call | tf_op jit(solution)/shard_map/pallas_call | solution.py:109
  98.4 1.3 copy-done.3
  99.7 11.1 %shard_map.58 = (bf16[12,384,128]{2,1,0:T(8,128)(2,1)S(1)}, bf16[16,12,8,384]{3,2,1,0:T(8,128)(2,1)S(1)}, bf16[16,12,8,384]{3,2,1,0:T(8,128)(2,1)S(1)}) custom-call(bf16[12,384,128]{2,1,0:T(8,128)(2,1)S(1)} %copy-done.2, f32[12,384]{1,0:T(8,128)S(1)} %multiply_multiply_fusion.mask_ref, bf16[128,640]{1,0:T(8,128)(2,1)S(1)} %get-tuple-element.24.w_ref, ...), custom_call_target="tpu_custom_call" | custom-call | tf_op jit(solution)/shard_map/pallas_call | solution.py:182
  110.8 1.0 copy-done.4
  111.8 1.0 copy-done.5
  112.9 32.6 %shard_map.59 = (bf16[16,12,8,384]{3,2,1,0:T(8,128)(2,1)}, bf16[16,12,8,384]{3,2,1,0:T(8,128)(2,1)}) custom-call(bf16[16,12,8,384]{3,2,1,0:T(8,128)(2,1)} %copy-done.4, bf16[16,12,8,384]{3,2,1,0:T(8,128)(2,1)} %copy-done.5), custom_call_target="tpu_custom_call" | custom-call | tf_op jit(solution)/shard_map/pallas_call | solution.py:109
  145.5 3.5 %fusion = bf16[384,8,384]{2,0,1:T(8,128)(2,1)S(1)} fusion(bf16[16,12,8,384]{3,2,1,0:T(8,128)(2,1)} %get-tuple-element.22, bf16[16,12,8,384]{3,2,1,0:T(8,128)(2,1)} %get-tuple-element.21), kind=kOutput, calls=%fused_computation.1 | convolution fusion | flops 454164480 | bytes 4718592 | tf_op jit(solution)/shard_map/srci,srcj->icj/dot_general | solution.py:221
  149.0 2.8 %copy.11 = bf16[384,8,384]{2,1,0:T(8,128)(2,1)} copy(bf16[384,8,384]{2,0,1:T(8,128)(2,1)S(1)} %fusion) | data formatting | bytes 4718592 | tf_op jit(solution)/shard_map/convert_element_type | solution.py:222
  151.9 59.1 %shard_map.60.tri_ref = bf16[32,12,8,384]{3,2,1,0:T(8,128)(2,1)} custom-call(bf16[32,12,8,384]{3,2,1,0:T(8,128)(2,1)} %bitcast.21), custom_call_target="tpu_custom_call" | custom-call | tf_op jit(solution)/shard_map/pallas_call | solution.py:109
  211.0 1.7 copy-done
  212.6 5.6 %shard_map.61 = bf16[12,384,128]{2,1,0:T(8,128)(2,1)} custom-call(bf16[12,384,128]{2,1,0:T(8,128)(2,1)S(1)} %get-tuple-element.18.state_ref, bf16[128,640]{1,0:T(8,128)(2,1)S(1)} %get-tuple-element.23.w_next_ref.w_ref, bf16[128,128]{1,0:T(8,128)(2,1)S(1)} %get-tuple-element.25.wo_ref, bf16[32,12,8,384]{3,2,1,0:T(8,128)(2,1)S(1)} %copy-done), custom_call_target="tpu_custom_call" | custom-call | tf_op jit(solution)/shard_map/pallas_call | solution.py:182
  (10 shorter events, 0.0 us)
Async XLA Ops:
  3.3 1.3 copy-start.1
  10.0 1.0 copy-start.6
  11.0 1.0 copy-start.7
  79.3 19.1 %copy-start.8 = (bf16[2,128,128]{2,1,0:T(8,128)(2,1)S(1)}, bf16[2,128,128]{2,1,0:T(8,128)(2,1)}, u32[]{:S(2)}) copy-start(bf16[2,128,128]{2,1,0:T(8,128)(2,1)} %param.9) | copy-start | bytes 196612
  79.3 19.1 %copy-start.2 = (bf16[12,384,128]{2,1,0:T(8,128)(2,1)S(1)}, bf16[12,384,128]{2,1,0:T(8,128)(2,1)}, u32[]{:S(2)}) copy-start(bf16[12,384,128]{2,1,0:T(8,128)(2,1)} %state_ref.3) | copy-start | bytes 3538948
  98.4 1.3 copy-start.3
  110.8 1.0 copy-start.4
  111.8 1.0 copy-start.5
  211.0 1.7 copy-start

commit v3 on v0

v3 whole, which is shorter than its diff:
```python
import functools

import jax
import jax.numpy as jnp
from jax import lax
from jax.experimental import pallas as pl
from jax.experimental.pallas import tpu as pltpu
from jax.sharding import PartitionSpec as P

EPS = 1e-05
MESH = pl.DeviceIdType.MESH


def norm_axis(values, axis):
    mean = jnp.mean(values, axis=axis, keepdims=True)
    centred = values - mean
    var = jnp.mean(centred * centred, axis=axis, keepdims=True)
    return centred * lax.rsqrt(var + EPS)


def dot(a, b, dims):
    return lax.dot_general(a, b, (dims, ((), ())), preferred_element_type=jnp.float32)


class Net:
    def __init__(self, n, wide):
        self.n, self.h, self.wide = n, n // 2, wide
        self.g = lax.axis_index("groups")
        self.me = lax.axis_index("row")
        self.half, self.q, self.core = self.me // self.h, self.me % self.h, self.me % 2

    def greet(self):
        barrier = pltpu.get_barrier_semaphore()

        def signal(dest):
            pl.semaphore_signal(
                barrier, inc=1, device_id=(self.g, dest), device_id_type=MESH
            )

        def near(s, carry):
            signal(self.half * self.h + (self.q + s) % self.h)
            return carry

        def far(s, carry):
            signal((1 - self.half) * self.h + (self.q + s) % self.h)
            return carry

        lax.fori_loop(1, self.h, near, 0)
        if self.wide:
            lax.fori_loop(0, self.h, far, 0)

    def met(self):
        pl.semaphore_wait(pltpu.get_barrier_semaphore(), (self.n if self.wide else self.h) - 1)


class Swap:
    def __init__(self, net, kind, src, dst, sems, step):
        self.net, self.kind, self.src, self.dst, self.step = net, kind, src, dst, step
        self.send_sem, self.recv_sem, self.own_sem = sems
        self.slot = net.q if kind == "half" else net.me
        self.count = net.h if kind == "half" else net.n

    def rows(self, t):
        return pl.ds(t * self.step, self.step)

    def block(self, to, dest):
        return dest if self.kind == "all" else to

    def send(self, t, to, dest):
        pltpu.make_async_remote_copy(
            src_ref=self.src.at[self.block(to, dest), self.rows(t)],
            dst_ref=self.dst.at[self.slot, self.rows(t)],
            send_sem=self.send_sem,
            recv_sem=self.recv_sem.at[t],
            device_id=(self.net.g, dest),
            device_id_type=MESH,
        ).start()

    def own(self, t):
        net = self.net
        return pltpu.make_async_copy(
            self.src.at[self.block(net.q, net.me), self.rows(t)],
            self.dst.at[self.slot, self.rows(t)],
            self.own_sem.at[t],
        )

    def arrived(self, t):
        self.own(t).wait()
        got = self.dst.at[pl.ds(0, self.count - 1), self.rows(t)]
        pltpu.make_async_copy(got, got, self.recv_sem.at[t]).wait()

    def sent(self):
        gone = self.dst.at[pl.ds(0, self.count - 1)]
        pltpu.make_async_copy(gone, gone, self.send_sem).wait()


def send_rows(net, swaps, t):
    h = net.h

    def step(s, carry):
        to = (net.q + s) % h if h & (h - 1) else net.q ^ s ^ (net.core * (h - 2))
        for swap in swaps:
            if swap.kind != "half":
                swap.send(t, to, (1 - net.half) * h + to)

        @pl.when(to != net.q)
        def _():
            for swap in swaps:
                swap.send(t, to, net.half * h + to)

        return carry

    for swap in swaps:
        swap.own(t).start()
    lax.fori_loop(0, h, step, 0)


def normed_row(state_ref, r):
    return norm_axis(state_ref[r].astype(jnp.float32), -1).astype(jnp.bfloat16)


def project_row(normed, u, w_ref, pair_mask_ref, token_mask_ref, left_ref, right_ref, r):
    owners, rows, share, tokens = left_ref.shape
    width = owners * share
    token = lax.axis_index("row") * rows + r
    columns = token_mask_ref[...]
    here = lax.broadcasted_iota(jnp.int32, (1, tokens), 1) == token
    row_token = jnp.sum(jnp.where(here, columns, 0.0), axis=1, keepdims=True)
    mask = pair_mask_ref[pl.ds(r, 1), :].astype(jnp.float32) * row_token * columns
    for lo, out_ref in ((0, left_ref), (2 * width, right_ref)):
        proj = dot(w_ref[u, :, lo : lo + 2 * width], normed, ((0,), (1,)))
        side = (mask * jax.nn.sigmoid(proj[:width]) * proj[width:]).astype(out_ref.dtype)
        for owner in range(owners):
            out_ref[owner, r] = side[owner * share : (owner + 1) * share]


def finish_row(state_ref, u, w_ref, wo_ref, tri_ref, r):
    sources, _, share, _ = tri_ref.shape
    width = wo_ref.shape[1]
    owners = width // share
    normed = normed_row(state_ref, r)
    tri = jnp.concatenate([tri_ref[s, r].astype(jnp.float32) for s in range(owners)], axis=0)
    if sources > owners:
        tri += jnp.concatenate(
            [tri_ref[s, r].astype(jnp.float32) for s in range(owners, sources)], axis=0
        )
    tri_normed = norm_axis(tri, 0).astype(jnp.bfloat16)
    out = dot(tri_normed, wo_ref[u], ((0,), (0,)))
    gate = jax.nn.sigmoid(dot(normed, w_ref[u, :, 4 * width :], ((1,), (0,))))
    return (state_ref[r].astype(jnp.float32) + gate * out).astype(jnp.bfloat16)


def each_row(t, step, body):
    def row(r, carry):
        body(r)
        return carry

    lax.fori_loop(t * step, (t + 1) * step, row, 0)


def first_kernel(n, step, state, pair_mask, token_mask, w, left, right, left_src, right_src, *sems):
    net = Net(n, True)
    swaps = [
        Swap(net, "half", left_src, left, sems[:3], step),
        Swap(net, "both", right_src, right, sems[3:], step),
    ]
    parts = state.shape[0] // step
    net.greet()
    for t in range(parts):
        each_row(
            t,
            step,
            lambda r: project_row(
                normed_row(state, r), 0, w, pair_mask, token_mask, left_src, right_src, r
            ),
        )
        if t == 0:
            net.met()
        send_rows(net, swaps, t)
    for swap in swaps:
        for t in range(parts):
            swap.arrived(t)
        swap.sent()


def middle_kernel(
    n, step, state, pair_mask, token_mask, w, wo, tri_src, after, left, right, tri, left_src, right_src, *sems
):
    net = Net(n, False)
    tri_swap = Swap(net, "half", tri_src, tri, sems[:3], step)
    swaps = [
        Swap(net, "half", left_src, left, sems[3:6], step),
        Swap(net, "half", right_src, right, sems[6:], step),
    ]
    parts = state.shape[0] // step
    net.greet()
    net.met()
    for t in range(parts):
        send_rows(net, [tri_swap], t)

    def body(r):
        after[r] = finish_row(state, 0, w, wo, tri, r)
        project_row(normed_row(after, r), 1, w, pair_mask, token_mask, left_src, right_src, r)

    for t in range(parts):
        tri_swap.arrived(t)
        each_row(t, step, body)
        send_rows(net, swaps, t)
    tri_swap.sent()
    for swap in swaps:
        for t in range(parts):
            swap.arrived(t)
        swap.sent()


def last_kernel(n, step, state, w, wo, tri_src, after, tri, *sems):
    net = Net(n, True)
    swap = Swap(net, "all", tri_src, tri, sems, step)
    parts = state.shape[0] // step
    net.greet()
    net.met()
    for t in range(parts):
        send_rows(net, [swap], t)

    def body(r):
        after[r] = finish_row(state, 1, w, wo, tri, r)

    for t in range(parts):
        swap.arrived(t)
        each_row(t, step, body)
    swap.sent()


def call(body, ident, n, step, swaps, args, outs, scratch):
    vmem = pl.BlockSpec(memory_space=pltpu.VMEM)
    parts = args[0].shape[0] // step
    dma = pltpu.SemaphoreType.DMA
    return pl.pallas_call(
        functools.partial(body, n, step),
        out_shape=[jax.ShapeDtypeStruct(shape, jnp.bfloat16) for shape in outs],
        in_specs=[vmem] * len(args),
        out_specs=[vmem] * len(outs),
        scratch_shapes=[pltpu.VMEM(shape, jnp.bfloat16) for shape in scratch]
        + [dma, dma((parts,)), dma((parts,))] * swaps,
        compiler_params=pltpu.CompilerParams(
            collective_id=ident, has_side_effects=True, vmem_limit_bytes=28 * 2**20
        ),
    )(*args)


def on_device(pair, pair_mask, token_mask, w, wo):
    rows, tokens, _ = pair.shape
    n = lax.axis_size("row")
    h = n // 2
    share = wo.shape[1] // h
    step = 4 if rows % 4 == 0 else rows
    cols = token_mask.astype(jnp.float32)[None, :]
    near, full = (h, rows, share, tokens), (n, rows, share, tokens)

    left, right = call(
        first_kernel, 1, n, step, 2, (pair, pair_mask, cols, w), (near, full), (near, near)
    )
    left = left.reshape(h * rows, share, tokens)
    right = right.reshape(tokens, share, tokens)
    tri = jnp.einsum("ick,jck->icj", left, right, preferred_element_type=jnp.float32)
    tri = tri.astype(jnp.bfloat16).reshape(near)
    state, left, right = call(
        middle_kernel,
        2,
        n,
        step,
        3,
        (pair, pair_mask, cols, w, wo, tri),
        (pair.shape, near, near),
        (near, near, near),
    )
    left = left.reshape(h * rows, share, tokens)
    right = right.reshape(h * rows, share, tokens)
    tri = jnp.einsum("kci,kcj->icj", left, right, preferred_element_type=jnp.float32)
    tri = tri.astype(jnp.bfloat16).reshape(full)
    return call(last_kernel, 3, n, step, 1, (state, w, wo, tri), (pair.shape,), (full,))[0]


def solution(mesh):
    return jax.shard_map(
        on_device,
        mesh=mesh,
        in_specs=(
            P(("groups", "row"), None, None),
            P(("groups", "row"), None),
            P("groups"),
            P(),
            P(),
        ),
        out_specs=P(("groups", "row"), None, None),
        check_vma=False,
    )
```

time: 243 us -> 169 us (0.70)
  Pallas kernels: 0 us -> 159 us
  waiting for transfers between devices: 103 us -> 0 us
  blocking collectives: 68.2 us -> 0 us
  local copies, waits for them, and re-layouts: 28 us -> 6.23 us
  starting transfers between devices: 16.8 us -> 0 us
  matrix products: 17.9 us -> 2.2 us
  other arithmetic: 7.79 us -> 0.68 us
    pallas_call x0 -> x3, Pallas kernels: none -> 159 us  [call(): pl.pallas_call(functools.partial(body, n, step), out_shape=[jax.ShapeDtyp...]
    all_to_all x4 -> x0, waiting for transfers between devices: 103 us -> none  [the longest x2 52.3 us: triangle_update(): lax.all_to_all(tri, 'row', split_axis=1, concat_axis=0, tiled=True)]
    all_to_all x2 -> x0, blocking collectives: 68.2 us -> none  [triangle_update(): lax.all_to_all(grouped_right, 'row', split_axis=0, concat_axis=2, tiled=T...]
    all_to_all x4 -> x0, starting transfers between devices: 16.8 us -> none  [the longest x2 11.1 us: triangle_update(): lax.all_to_all(grouped_left, 'row', split_axis=0, concat_axis=2, tiled=True)]
    dot_general x8 -> x2, matrix products: 17.9 us -> 2.2 us  [the longest x1 1.12 us: on_device(): jnp.einsum('kci,kcj->icj', left, right, preferred_element_type=jnp.float32)]
    reshape x8 -> x0, local copies, waits for them, and re-layouts: 13.5 us -> none  [the longest x4 7.83 us: triangle_update(): grouped_left = left.reshape(owners, width // owners, rows, tokens)]
    convert_element_type x11 -> x2, local copies, waits for them, and re-layouts: 11.2 us -> 2.08 us  [the longest x1 1.39 us: on_device(): tri = tri.astype(jnp.bfloat16).reshape(full)]
    convert_element_type x6 -> x1, other arithmetic: 4.22 us -> 0.68 us  [on_device(): cols = token_mask.astype(jnp.float32)[None, :]]
  transfers between devices with their start and end apart: 4 -> 0, of which waited for: 4 -> 0; matrix products, arithmetic and copies ran while one was open for 5% -> 0% of each run, Pallas kernels for 0% -> 0%
where the time goes in v3:
time: 169 us
  Pallas kernels  159 us (94%)
  local copies, waits for them, and re-layouts  6.23 us (4%)
  matrix products  2.2 us (1%)
    pallas_call x3, Pallas kernels, call(): pl.pallas_call(functools.partial(body, n, step), out_shape=[jax.ShapeDtyp...  159 us
    unnamed x11, local copies, waits for them, and re-layouts  4.14 us

profile of v3, /device:TPU:0, one launch (start us, length us, event | category | flops | bytes accessed | tf_op | source)
XLA Modules:
  0.0 168.5 jit_solution(14137717383974251392)
XLA Ops:
  0.0 0.7 convert_element_type.15
  0.7 0.0 copy-start
  0.7 1.3 copy-done
  2.0 0.0 copy-start.1
  2.0 1.0 copy-done.1
  2.9 0.0 copy-start.4
  2.9 0.7 copy-done.4
  3.7 59.0 %shard_map.55 = (bf16[16,12,8,384]{3,2,1,0:T(8,128)(2,1)S(1)}, bf16[32,12,8,384]{3,2,1,0:T(8,128)(2,1)S(1)}) custom-call(bf16[12,384,128]{2,1,0:T(8,128)(2,1)S(1)} %copy-done, s32[12,384]{1,0:T(8,128)S(1)} %copy-done.4, f32[1,384]{1,0:T(1,128)S(1)} %broadcast_in_dim.3.token_mask, bf16[2,128,640]{2,1,0:T(8,128)(2,1)S(1)} %copy-done.1), custom_call_target="tpu_custom_call" | custom-call | tf_op jit(solution)/shard_map/pallas_call | solution.py:238
  62.6 1.1 fusion.5
  63.7 0.0 copy-start.3
  63.7 0.7 copy.8
  64.4 0.1 copy-done.3
  64.6 43.4 %shard_map.56 = (bf16[12,384,128]{2,1,0:T(8,128)(2,1)S(1)}, bf16[16,12,8,384]{3,2,1,0:T(8,128)(2,1)S(1)}, bf16[16,12,8,384]{3,2,1,0:T(8,128)(2,1)S(1)}) custom-call(bf16[12,384,128]{2,1,0:T(8,128)(2,1)S(1)} %copy-done, s32[12,384]{1,0:T(8,128)S(1)} %copy-done.4, f32[1,384]{1,0:T(1,128)S(1)} %broadcast_in_dim.3.token_mask, ...), custom_call_target="tpu_custom_call" | custom-call | tf_op jit(solution)/shard_map/pallas_call | solution.py:238
  108.0 1.1 convert_bitcast_fusion
  109.1 0.0 copy-start.2
  109.1 1.4 copy.11
  110.5 0.0 copy-done.2
  110.5 57.0 %shard_map.57 = bf16[12,384,128]{2,1,0:T(8,128)(2,1)S(1)} custom-call(bf16[12,384,128]{2,1,0:T(8,128)(2,1)S(1)} %get-tuple-element.12.state, bf16[2,128,640]{2,1,0:T(8,128)(2,1)S(1)} %copy-done.2, bf16[2,128,128]{2,1,0:T(8,128)(2,1)S(1)} %copy-done.3, bf16[32,12,8,384]{3,2,1,0:T(8,128)(2,1)S(1)} %bitcast.10), custom_call_target="tpu_custom_call" | custom-call | tf_op jit(solution)/shard_map/pallas_call | solution.py:238
  167.5 1.0 copy.25
  (1 shorter events, 0.0 us)
Async XLA Ops:
  0.7 1.3 copy-start
  2.0 1.0 copy-start.1
  2.9 0.7 copy-start.4
  63.7 0.8 copy-start.3
  109.1 1.4 copy-start.2

commit v4 on v3

--- a/solution.py
+++ b/solution.py
@@ -9,6 +9,7 @@
 
 EPS = 1e-05
 MESH = pl.DeviceIdType.MESH
+FIRST, MIDDLE, LAST = (4, 4, 4), (1, 1, 2, 2, 3, 3), (6, 4, 2)
 
 
 def norm_axis(values, axis):
@@ -20,6 +21,12 @@
 
 def dot(a, b, dims):
     return lax.dot_general(a, b, (dims, ((), ())), preferred_element_type=jnp.float32)
+
+
+def cut(rows, sizes):
+    if sum(sizes) != rows:
+        return ((0, rows),)
+    return tuple((sum(sizes[:t]), size) for t, size in enumerate(sizes))
 
 
 class Net:
@@ -54,14 +61,14 @@
 
 
 class Swap:
-    def __init__(self, net, kind, src, dst, sems, step):
-        self.net, self.kind, self.src, self.dst, self.step = net, kind, src, dst, step
+    def __init__(self, net, kind, src, dst, sems, parts):
+        self.net, self.kind, self.src, self.dst, self.parts = net, kind, src, dst, parts
         self.send_sem, self.recv_sem, self.own_sem = sems
         self.slot = net.q if kind == "half" else net.me
         self.count = net.h if kind == "half" else net.n
 
     def rows(self, t):
-        return pl.ds(t * self.step, self.step)
+        return pl.ds(*self.parts[t])
 
     def block(self, to, dest):
         return dest if self.kind == "all" else to
@@ -119,19 +126,22 @@
     return norm_axis(state_ref[r].astype(jnp.float32), -1).astype(jnp.bfloat16)
 
 
-def project_row(normed, u, w_ref, pair_mask_ref, token_mask_ref, left_ref, right_ref, r):
-    owners, rows, share, tokens = left_ref.shape
-    width = owners * share
+def mask_row(pair_mask_ref, token_mask_ref, r):
+    rows, tokens = pair_mask_ref.shape
     token = lax.axis_index("row") * rows + r
-    columns = token_mask_ref[...]
+    columns = token_mask_ref[...].astype(jnp.float32)
     here = lax.broadcasted_iota(jnp.int32, (1, tokens), 1) == token
     row_token = jnp.sum(jnp.where(here, columns, 0.0), axis=1, keepdims=True)
-    mask = pair_mask_ref[pl.ds(r, 1), :].astype(jnp.float32) * row_token * columns
-    for lo, out_ref in ((0, left_ref), (2 * width, right_ref)):
-        proj = dot(w_ref[u, :, lo : lo + 2 * width], normed, ((0,), (1,)))
-        side = (mask * jax.nn.sigmoid(proj[:width]) * proj[width:]).astype(out_ref.dtype)
-        for owner in range(owners):
-            out_ref[owner, r] = side[owner * share : (owner + 1) * share]
+    return pair_mask_ref[pl.ds(r, 1), :].astype(jnp.float32) * row_token * columns
+
+
+def project_row(normed, w, mask, out_ref, r):
+    owners, _, share, _ = out_ref.shape
+    proj = dot(w, normed, ((0,), (1,)))
+    half = owners * share
+    side = (mask * jax.nn.sigmoid(proj[:half]) * proj[half:]).astype(out_ref.dtype)
+    for owner in range(owners):
+        out_ref[owner, r] = side[owner * share : (owner + 1) * share]
 
 
 def finish_row(state_ref, u, w_ref, wo_ref, tri_ref, r):
@@ -150,98 +160,93 @@
     return (state_ref[r].astype(jnp.float32) + gate * out).astype(jnp.bfloat16)
 
 
-def each_row(t, step, body):
+def each_row(part, body):
     def row(r, carry):
         body(r)
         return carry
 
-    lax.fori_loop(t * step, (t + 1) * step, row, 0)
-
-
-def first_kernel(n, step, state, pair_mask, token_mask, w, left, right, left_src, right_src, *sems):
+    lax.fori_loop(part[0], part[0] + part[1], row, 0)
+
+
+def first_kernel(n, parts, state, pair_mask, token_mask, w, left, right, left_src, right_src, *sems):
     net = Net(n, True)
     swaps = [
-        Swap(net, "half", left_src, left, sems[:3], step),
-        Swap(net, "both", right_src, right, sems[3:], step),
+        Swap(net, "half", left_src, left, sems[:3], parts),
+        Swap(net, "both", right_src, right, sems[3:], parts),
     ]
-    parts = state.shape[0] // step
+    width = left.shape[0] * left.shape[2]
     net.greet()
-    for t in range(parts):
-        each_row(
-            t,
-            step,
-            lambda r: project_row(
-                normed_row(state, r), 0, w, pair_mask, token_mask, left_src, right_src, r
-            ),
-        )
+
+    def body(r):
+        normed = normed_row(state, r)
+        mask = mask_row(pair_mask, token_mask, r)
+        project_row(normed, w[0, :, : 2 * width], mask, left_src, r)
+        project_row(normed, w[0, :, 2 * width : 4 * width], mask, right_src, r)
+
+    for t in range(len(parts)):
+        each_row(parts[t], body)
         if t == 0:
             net.met()
         send_rows(net, swaps, t)
     for swap in swaps:
-        for t in range(parts):
+        for t in range(len(parts)):
             swap.arrived(t)
         swap.sent()
 
 
 def middle_kernel(
-    n, step, state, pair_mask, token_mask, w, wo, tri_src, after, left, right, tri, left_src, right_src, *sems
+    n, parts, state, pair_mask, token_mask, w, wo, w_next, tri_src, after, sides, tri, sides_src, *sems
 ):
-    net = Net(n, False)
-    tri_swap = Swap(net, "half", tri_src, tri, sems[:3], step)
-    swaps = [
-        Swap(net, "half", left_src, left, sems[3:6], step),
-        Swap(net, "half", right_src, right, sems[6:], step),
-    ]
-    parts = state.shape[0] // step
+    net = Net(n, True)
+    tri_swap = Swap(net, "half", tri_src, tri, sems[:3], parts)
+    sides_swap = Swap(net, "all", sides_src, sides, sems[3:], parts)
     net.greet()
     net.met()
-    for t in range(parts):
+    for t in range(len(parts)):
         send_rows(net, [tri_swap], t)
 
     def body(r):
         after[r] = finish_row(state, 0, w, wo, tri, r)
-        project_row(normed_row(after, r), 1, w, pair_mask, token_mask, left_src, right_src, r)
-
-    for t in range(parts):
+        mask = mask_row(pair_mask, token_mask, r)
+        project_row(normed_row(after, r), w_next[...], mask, sides_src, r)
+
+    for t in range(len(parts)):
         tri_swap.arrived(t)
-        each_row(t, step, body)
-        send_rows(net, swaps, t)
+        each_row(parts[t], body)
+        send_rows(net, [sides_swap], t)
     tri_swap.sent()
-    for swap in swaps:
-        for t in range(parts):
-            swap.arrived(t)
-        swap.sent()
-
-
-def last_kernel(n, step, state, w, wo, tri_src, after, tri, *sems):
+    for t in range(len(parts)):
+        sides_swap.arrived(t)
+    sides_swap.sent()
+
+
+def last_kernel(n, parts, state, w, wo, tri_src, after, tri, *sems):
     net = Net(n, True)
-    swap = Swap(net, "all", tri_src, tri, sems, step)
-    parts = state.shape[0] // step
+    swap = Swap(net, "all", tri_src, tri, sems, parts)
     net.greet()
     net.met()
-    for t in range(parts):
+    for t in range(len(parts)):
         send_rows(net, [swap], t)
 
     def body(r):
         after[r] = finish_row(state, 1, w, wo, tri, r)
 
-    for t in range(parts):
+    for t in range(len(parts)):
         swap.arrived(t)
-        each_row(t, step, body)
+        each_row(parts[t], body)
     swap.sent()
 
 
-def call(body, ident, n, step, swaps, args, outs, scratch):
+def call(body, ident, n, parts, swaps, args, outs, scratch):
     vmem = pl.BlockSpec(memory_space=pltpu.VMEM)
-    parts = args[0].shape[0] // step
     dma = pltpu.SemaphoreType.DMA
     return pl.pallas_call(
-        functools.partial(body, n, step),
+        functools.partial(body, n, parts),
         out_shape=[jax.ShapeDtypeStruct(shape, jnp.bfloat16) for shape in outs],
         in_specs=[vmem] * len(args),
         out_specs=[vmem] * len(outs),
         scratch_shapes=[pltpu.VMEM(shape, jnp.bfloat16) for shape in scratch]
-        + [dma, dma((parts,)), dma((parts,))] * swaps,
+        + [dma, dma((len(parts),)), dma((len(parts),))] * swaps,
         compiler_params=pltpu.CompilerParams(
             collective_id=ident, has_side_effects=True, vmem_limit_bytes=28 * 2**20
         ),
@@ -252,33 +257,39 @@
     rows, tokens, _ = pair.shape
     n = lax.axis_size("row")
     h = n // 2
-    share = wo.shape[1] // h
-    step = 4 if rows % 4 == 0 else rows
-    cols = token_mask.astype(jnp.float32)[None, :]
+    width = wo.shape[1]
+    share, part = width // h, width // n
+    cols = token_mask[None, :]
     near, full = (h, rows, share, tokens), (n, rows, share, tokens)
+    packed, slim = (n, rows, 2 * part, tokens), (n, rows, part, tokens)
+    w_next = w[1, :, : 4 * width].reshape(-1, 2, 2, n, part).transpose(0, 2, 3, 1, 4)
+    w_next = w_next.reshape(-1, 4 * width)
 
     left, right = call(
-        first_kernel, 1, n, step, 2, (pair, pair_mask, cols, w), (near, full), (near, near)
+        first_kernel, 1, n, cut(rows, FIRST), 2, (pair, pair_mask, cols, w), (near, full), (near, near)
     )
     left = left.reshape(h * rows, share, tokens)
     right = right.reshape(tokens, share, tokens)
     tri = jnp.einsum("ick,jck->icj", left, right, preferred_element_type=jnp.float32)
     tri = tri.astype(jnp.bfloat16).reshape(near)
-    state, left, right = call(
+    state, sides = call(
         middle_kernel,
         2,
         n,
-        step,
-        3,
-        (pair, pair_mask, cols, w, wo, tri),
-        (pair.shape, near, near),
-        (near, near, near),
+        cut(rows, MIDDLE),
+        2,
+        (pair, pair_mask, cols, w, wo, w_next, tri),
+        (pair.shape, packed),
+        (near, packed),
     )
-    left = left.reshape(h * rows, share, tokens)
-    right = right.reshape(h * rows, share, tokens)
-    tri = jnp.einsum("kci,kcj->icj", left, right, preferred_element_type=jnp.float32)
-    tri = tri.astype(jnp.bfloat16).reshape(full)
-    return call(last_kernel, 3, n, step, 1, (state, w, wo, tri), (pair.shape,), (full,))[0]
+    sides = sides.reshape(tokens, 2 * part, tokens)
+    tri = jnp.einsum(
+        "kci,kcj->icj", sides[:, :part], sides[:, part:], preferred_element_type=jnp.float32
+    )
+    tri = tri.astype(jnp.bfloat16).reshape(slim)
+    return call(
+        last_kernel, 3, n, cut(rows, LAST), 1, (state, w, wo, tri), (pair.shape,), (slim,)
+    )[0]
 
 
 def solution(mesh):

time: 169 us -> 162 us (0.959)
  Pallas kernels: 159 us -> 152 us
    pallas_call x3, Pallas kernels: 159 us -> 152 us  [call(): pl.pallas_call(functools.partial(body, n, parts), out_shape=[jax.ShapeDty...]
    unnamed x11 -> x10, local copies, waits for them, and re-layouts: 4.14 us -> 3.28 us
where the time goes in v4:
time: 162 us
  Pallas kernels  152 us (94%)
  local copies, waits for them, and re-layouts  7.45 us (5%)
  matrix products  2.04 us (1%)
    pallas_call x3, Pallas kernels, call(): pl.pallas_call(functools.partial(body, n, parts), out_shape=[jax.ShapeDty...  152 us
    unnamed x10, local copies, waits for them, and re-layouts  3.28 us

profile of v4, /device:TPU:0, one launch (start us, length us, event | category | flops | bytes accessed | tf_op | source)
XLA Modules:
  0.0 162.1 jit_solution(1892828038473911068)
XLA Ops:
  0.0 0.0 copy-start.1
  0.0 0.7 broadcast_in_dim.3.token_mask
  0.7 0.9 slice.9
  1.6 0.1 copy.22
  1.8 0.1 copy.18.w_next
  2.0 0.0 copy-done.1
  2.0 0.0 copy-start
  2.0 1.3 copy-done
  3.2 0.0 copy-start.3
  3.2 0.7 copy-done.3
  4.0 59.0 %shard_map.55 = (bf16[16,12,8,384]{3,2,1,0:T(8,128)(2,1)S(1)}, bf16[32,12,8,384]{3,2,1,0:T(8,128)(2,1)S(1)}) custom-call(bf16[12,384,128]{2,1,0:T(8,128)(2,1)S(1)} %copy-done, s32[12,384]{1,0:T(8,128)S(1)} %copy-done.3, s32[1,384]{1,0:T(1,128)S(1)} %broadcast_in_dim.3.token_mask, bf16[2,128,640]{2,1,0:T(8,128)(2,1)S(1)} %copy-done.1), custom_call_target="tpu_custom_call" | custom-call | tf_op jit(solution)/shard_map/pallas_call | solution.py:243
  62.9 1.1 fusion.5
  64.0 0.0 copy-start.2
  64.0 0.7 copy.17
  64.7 0.1 copy-done.2
  64.9 61.8 %shard_map.56 = (bf16[12,384,128]{2,1,0:T(8,128)(2,1)S(1)}, bf16[32,12,8,384]{3,2,1,0:T(8,128)(2,1)S(1)}) custom-call(bf16[12,384,128]{2,1,0:T(8,128)(2,1)S(1)} %copy-done, s32[12,384]{1,0:T(8,128)S(1)} %copy-done.3, s32[1,384]{1,0:T(1,128)S(1)} %broadcast_in_dim.3.token_mask, bf16[2,128,640]{2,1,0:T(8,128)(2,1)S(1)} %copy-done.1, ...), custom_call_target="tpu_custom_call" | custom-call | tf_op jit(solution)/shard_map/pallas_call | solution.py:243
  126.6 0.8 fusion.12
  127.4 1.0 fusion.8
  128.4 0.9 copy.21
  129.3 31.7 %shard_map.57 = bf16[12,384,128]{2,1,0:T(8,128)(2,1)S(1)} custom-call(bf16[12,384,128]{2,1,0:T(8,128)(2,1)S(1)} %get-tuple-element.11.state, bf16[2,128,640]{2,1,0:T(8,128)(2,1)S(1)} %copy-done.1, bf16[2,128,128]{2,1,0:T(8,128)(2,1)S(1)} %copy-done.2, bf16[32,12,4,384]{3,2,1,0:T(4,128)(2,1)S(1)} %bitcast.14), custom_call_target="tpu_custom_call" | custom-call | tf_op jit(solution)/shard_map/pallas_call | solution.py:243
  161.1 1.0 copy.38
  (1 shorter events, 0.0 us)
Async XLA Ops:
  0.0 2.0 %copy-start.1 = (bf16[2,128,640]{2,1,0:T(8,128)(2,1)S(1)}, bf16[2,128,640]{2,1,0:T(8,128)(2,1)}, u32[]{:S(2)}) copy-start(bf16[2,128,640]{2,1,0:T(8,128)(2,1)} %w.5) | copy-start | bytes 983044
  2.0 1.3 copy-start
  3.2 0.7 copy-start.3
  64.0 0.8 copy-start.2
